TPU v7x, 32 devices: a whole 2x2x4 slice. The times are simulated.
32 devices in a mesh: row: 8 (over z, core), col: 4 (over y, x).
Axes of the slice: x: 2, y: 2, z: 4, core: 2. Of those that a mesh axis runs over, the one named last changes fastest.
Arguments:
- hidden_pre: bfloat16 [512, 16384], P('col', 'row'), may hold values from -6 to 6
- weight_blocks: bfloat16 [8, 4, 8, 256, 256], P('row', 'col'), may hold values from -0.09375 to 0.09375
- block_rows: int32 [8, 4, 8], P('row', 'col'), may hold values from 0 to 63, as said below
- block_cols: int32 [8, 4, 8], P('row', 'col'), may hold values from 0 to 31, as said below
- block_counts: int32 [8, 4], P('row', 'col'), may hold values from 2 to 8, as said below
- out_grad: bfloat16 [512, 8192], P('row', 'col'), may hold values from -6 to 6
Outputs:
- projected: bfloat16 [512, 8192], P('row', 'col')
- grad_hidden: bfloat16 [512, 16384], P('col', 'row')
- grad_blocks: float32 [8, 4, 8, 256, 256], P('row', 'col')
Inputs may be any that keep to these rules, and one draw needn't show every extreme that they name: `block_rows`: owner (r, c) holds only blocks of block-rows r * 8 to (r + 1) * 8 - 1 and block-columns c * 8 to (c + 1) * 8 - 1; the 8 slots of one owner name 8 different blocks. `block_cols`: same owner ranges as block_rows. `block_counts`: some owner holds exactly 8 live blocks and some owner exactly 2.
All inputs are finite; a program needn't handle non-finite values.
Results may differ from a plain program's by a relative error of at most 0.0051.
Values may be sent and summed in bfloat16 or wider, within the bound.
A program may use at most 128 MiB of HBM per device.

v0:
```python
import jax
import jax.numpy as jnp
from jax import lax
from jax.sharding import PartitionSpec as P


def silu_rounded(values):
    return jax.nn.silu(values.astype(jnp.float32)).astype(jnp.bfloat16)


def on_device(hidden_pre, weight_blocks, block_rows, block_cols, block_counts, out_grad):
    width = weight_blocks.shape[-1]
    slot_count = weight_blocks.shape[2]
    row_span = hidden_pre.shape[1] // width
    col_span = out_grad.shape[1] // width
    row_base = lax.axis_index("row") * row_span
    row_local = block_rows[0, 0] - row_base
    col_local = block_cols[0, 0] - lax.axis_index("col") * col_span
    alive = jnp.arange(slot_count, dtype=jnp.int32) < block_counts[0, 0]
    w_live = jnp.where(
        alive[:, None, None], weight_blocks[0, 0], jnp.zeros_like(weight_blocks[0, 0])
    )
    row_pick = (row_local[:, None] == jnp.arange(row_span, dtype=jnp.int32)[None, :]).astype(
        jnp.float32
    )
    col_pick = (col_local[:, None] == jnp.arange(col_span, dtype=jnp.int32)[None, :]).astype(
        jnp.float32
    )
    grad_full = lax.all_gather(out_grad, "row", axis=0, tiled=True)
    act_rows = silu_rounded(lax.all_gather(hidden_pre, "col", axis=0, tiled=True))
    count = act_rows.shape[0]
    a_stack = jnp.take(act_rows.reshape(count, row_span, width), row_local, axis=1)
    prod = jnp.einsum("nkp,kpq->nkq", a_stack, w_live, preferred_element_type=jnp.float32)
    placed = jnp.einsum("nkq,kc->ncq", prod, col_pick, precision=lax.Precision.HIGHEST)
    partial_value = placed.reshape(count, col_span * width)
    grad_rows = grad_full
    act_rows = silu_rounded(lax.all_gather(hidden_pre, "col", axis=0, tiled=True))
    count = act_rows.shape[0]
    a_stack = jnp.take(act_rows.reshape(count, row_span, width), row_local, axis=1)
    g_stack = jnp.take(grad_rows.reshape(count, col_span, width), col_local, axis=1)
    weight_grad = jnp.einsum("nkp,nkq->kpq", a_stack, g_stack, preferred_element_type=jnp.float32)
    projected = lax.psum_scatter(partial_value, "row", scatter_dimension=0, tiled=True).astype(
        jnp.bfloat16
    )
    count = hidden_pre.shape[0] * lax.axis_size("col")
    grad_rows = grad_full
    g_stack = jnp.take(grad_rows.reshape(count, col_span, width), col_local, axis=1)
    back = jnp.einsum("nkq,kpq->nkp", g_stack, w_live, preferred_element_type=jnp.float32)
    placed = jnp.einsum("nkp,kr->nrp", back, row_pick, precision=lax.Precision.HIGHEST)
    back_act = lax.psum_scatter(
        placed.reshape(count, row_span * width), "col", scatter_dimension=0, tiled=True
    )
    hidden_f = hidden_pre.astype(jnp.float32)
    sig = jax.nn.sigmoid(hidden_f)
    grad_hidden = (back_act * (sig * (1.0 + hidden_f * (1.0 - sig)))).astype(jnp.bfloat16)
    grad_blocks = jnp.where(alive[:, None, None], weight_grad, jnp.zeros_like(weight_grad))
    return (projected, grad_hidden, grad_blocks[None, None])


def solution(mesh):
    placed = (
        P("col", "row"),
        P("row", "col", None, None, None),
        P("row", "col", None),
        P("row", "col", None),
        P("row", "col"),
        P("row", "col"),
    )
    return jax.shard_map(
        on_device,
        mesh=mesh,
        in_specs=placed,
        out_specs=(P("row", "col"), P("col", "row"), P("row", "col", None, None, None)),
        check_vma=False,
    )
```

profile of v0, /device:TPU:0, one launch (start us, length us, event | category | flops | bytes accessed | tf_op | source)
XLA Modules:
  0.0 193.5 jit_solution(5066251066862516377)
XLA Ops:
  7.2 0.0 all-gather.3.cloned.1.call-start
  7.2 2.0 %copy.18 = bf16[128,2048]{0,1:T(8,128)(2,1)} copy(bf16[128,2048]{1,0:T(8,128)(2,1)} %param.8) | data formatting | bytes 1048576 | tf_op args[0]
  9.3 0.0 all-gather.3.cloned.1.call-update
  9.3 0.0 all-gather.5.cloned.1.call-start
  9.3 0.7 all-gather.5.cloned.1.call-update
  10.0 0.0 reduce-scatter.3.cloned.1.call-start
  10.7 0.7 compare_and_fusion.1
  11.4 0.7 compare_and_fusion
  12.1 36.2 %all-gather.3.cloned.1.call-done = bf16[512,2048]{0,1:T(8,128)(2,1)} async-done(((bf16[128,2048]{0,1:T(8,128)(2,1)}), bf16[512,2048]{0,1:T(8,128)(2,1)}) %all-gather.3.cloned.1.call-update) | async-done | bytes 2097168 | tf_op jit(solution)/shard_map/all_gather | solution.py:30
  48.3 4.1 %fusion.3 = bf16[512,2048]{0,1:T(8,128)(2,1)} fusion(bf16[512,2048]{0,1:T(8,128)(2,1)} %all-gather.3.cloned.1.call-done), kind=kLoop, calls=%fused_computation.7 | loop fusion | flops 6291456 | bytes 4194304 | tf_op jit(solution)/shard_map/convert_element_type | solution.py:8
  52.4 2.8 %copy.19 = bf16[512,8,256]{2,0,1:T(8,128)(2,1)S(1)} copy(bf16[512,8,256]{0,2,1:T(8,128)(2,1)} %bitcast.52) | data formatting | bytes 4194304 | tf_op jit(solution)/shard_map/reshape | solution.py:32
  55.2 0.0 copy-start.1
  55.2 2.0 %gather_fusion = bf16[8,512,256]{2,1,0:T(8,128)(2,1)} fusion(bf16[512,8,256]{2,0,1:T(8,128)(2,1)S(1)} %copy.19, s32[1024]{0:T(1024)S(1)} %pad_clamp_fusion.1), kind=kCustom, calls=%fused_computation.clone | custom fusion | bytes 4194336 | tf_op jit(solution)/shard_map/jit(_take)/gather | solution.py:32
  57.2 0.0 copy-done.1
  57.2 4.6 %convolution_bitcast_fusion.1 = f32[512,8,256]{0,2,1:T(8,128)} fusion(bf16[8,512,256]{2,1,0:T(8,128)(2,1)} %gather_fusion, pred[8]{0:T(512)(128)(4,1)S(1)} %get-tuple-element.6, bf16[1,1,8,256,256]{4,3,2,1,0:T(8,128)(2,1)S(1)} %copy-done.1, pred[8]{0:T(512)(128)(4,1)S(1)} %get-tuple-element.8), kind=kOutput, calls=%fused_computation.9 | convolution fusion | flops 538443776 | bytes 7340048 | tf_op jit(solution)/shard_map/nkp,kpq->nkq/dot_general | solution.py:33
  61.8 5.5 %copy.21 = f32[512,8,256]{2,1,0:T(8,128)} copy(f32[512,8,256]{0,2,1:T(8,128)} %convolution_bitcast_fusion.1) | data formatting | bytes 8388608 | tf_op jit(solution)/shard_map/nkp,kpq->nkq/transpose | solution.py:33
  67.3 4.3 %fusion.21 = f32[8,512,256]{2,0,1:T(8,128)S(1)} fusion(f32[512,8,256]{2,1,0:T(8,128)} %copy.21, s32[8]{0:T(128)S(1)} %get-tuple-element.5), kind=kOutput, calls=%fused_computation.33 | convolution fusion | flops 100663360 | bytes 8388640 | tf_op jit(solution)/shard_map/nkq,kc->ncq/dot_general | solution.py:34
  71.6 3.9 %copy.28 = f32[64,8,8,256]{3,1,2,0:T(8,128)} copy(f32[64,8,8,256]{3,2,1,0:T(8,128)S(1)} %bitcast.51) | data formatting | bytes 8388608
  75.5 0.0 reduce-scatter.3.cloned.1.call-update
  75.5 0.2 reduce-scatter.5.cloned.1.call-start
  75.8 3.3 %all-gather.5.cloned.1.call-done = bf16[512,2048]{1,0:T(8,128)(2,1)} async-done(((bf16[64,2048]{1,0:T(8,128)(2,1)}), bf16[512,2048]{1,0:T(8,128)(2,1)}) %all-gather.5.cloned.1.call-update) | async-done | bytes 2097168 | tf_op jit(solution)/shard_map/all_gather | solution.py:29
  79.0 3.9 %copy.22 = bf16[512,2048]{0,1:T(8,128)(2,1)} copy(bf16[512,2048]{1,0:T(8,128)(2,1)} %all-gather.5.cloned.1.call-done) | data formatting | bytes 4194304 | tf_op jit(solution)/shard_map/all_gather | solution.py:29
  82.9 2.8 %copy.23 = bf16[512,8,256]{2,0,1:T(8,128)(2,1)S(1)} copy(bf16[512,8,256]{0,2,1:T(8,128)(2,1)} %bitcast.53) | data formatting | bytes 4194304 | tf_op jit(solution)/shard_map/reshape | solution.py:47
  85.8 2.0 %gather_fusion.1 = bf16[8,512,256]{2,1,0:T(8,128)(2,1)} fusion(bf16[512,8,256]{2,0,1:T(8,128)(2,1)S(1)} %copy.23, s32[1024]{0:T(1024)S(1)} %pad_clamp_fusion), kind=kCustom, calls=%fused_computation.1.clone | custom fusion | bytes 4194336 | tf_op jit(solution)/shard_map/jit(_take)/gather | solution.py:47
  87.8 4.4 %convolution_bitcast_fusion = f32[512,8,256]{0,2,1:T(8,128)} fusion(bf16[8,512,256]{2,1,0:T(8,128)(2,1)} %gather_fusion.1, pred[8]{0:T(512)(128)(4,1)S(1)} %get-tuple-element.4, bf16[1,1,8,256,256]{4,3,2,1,0:T(8,128)(2,1)S(1)} %copy-done.1, pred[8]{0:T(512)(128)(4,1)S(1)} %get-tuple-element.8), kind=kOutput, calls=%fused_computation.8 | convolution fusion | flops 538443776 | bytes 7340048 | tf_op jit(solution)/shard_map/nkq,kpq->nkp/dot_general | solution.py:48
  92.2 5.5 %copy.24 = f32[512,8,256]{2,1,0:T(8,128)} copy(f32[512,8,256]{0,2,1:T(8,128)} %convolution_bitcast_fusion) | data formatting | bytes 8388608 | tf_op jit(solution)/shard_map/nkq,kpq->nkp/transpose | solution.py:48
  97.7 4.3 %fusion.24 = f32[8,512,256]{2,0,1:T(8,128)S(1)} fusion(f32[512,8,256]{2,1,0:T(8,128)} %copy.24, s32[8]{0:T(128)S(1)} %get-tuple-element.7), kind=kOutput, calls=%fused_computation.35 | convolution fusion | flops 100663360 | bytes 8388640 | tf_op jit(solution)/shard_map/nkp,kr->nrp/dot_general | solution.py:49
  101.9 3.9 %copy.29 = f32[64,8,8,256]{3,1,2,0:T(8,128)} copy(f32[64,8,8,256]{3,2,1,0:T(8,128)S(1)} %bitcast.50) | data formatting | bytes 8388608
  105.9 0.0 copy-start
  105.9 0.0 reduce-scatter.5.cloned.1.call-update
  105.9 1.6 copy-done
  107.5 0.0 copy-start.2
  107.5 4.0 %select_bitcast_fusion = f32[1,1,8,256,256]{4,3,2,1,0:T(8,128)} fusion(pred[8]{0:T(512)(128)(4,1)S(1)} %get-tuple-element.8, bf16[8,512,256]{2,1,0:T(8,128)(2,1)S(1)} %copy-done, pred[8]{0:T(512)(128)(4,1)S(1)} %get-tuple-element.6, bf16[8,512,256]{2,1,0:T(8,128)(2,1)} %gather_fusion.1, pred[8]{0:T(512)(128)(4,1)S(1)} %get-tuple-element.4), kind=kOutput, calls=%fused_computation.15 | convolution fusion | flops 539492352 | bytes 6291480 | tf_op jit(solution)/shard_map/nkp,nkq->kpq/dot_general | solution.py:41
  111.5 19.4 %reduce-scatter.3.cloned.1.call-done = f32[64,2048]{1,0:T(8,128)} async-done(((f32[512,2048]{1,0:T(8,128)}), f32[64,2048]{1,0:T(8,128)}) %reduce-scatter.3.cloned.1.call-update) | async-done | bytes 524304 | tf_op jit(solution)/shard_map/reduce_scatter | solution.py:42
  130.9 1.8 convert_element_type.21
  132.7 51.9 %reduce-scatter.5.cloned.1.call-done = f32[128,2048]{1,0:T(8,128)} async-done(((f32[512,2048]{1,0:T(8,128)}), f32[128,2048]{1,0:T(8,128)}) %reduce-scatter.5.cloned.1.call-update) | async-done | bytes 1048592 | tf_op jit(solution)/shard_map/reduce_scatter | solution.py:50
  184.6 0.0 copy-done.2
  184.6 2.4 %fusion.19 = bf16[128,2048]{1,0:T(8,128)(2,1)} fusion(f32[128,2048]{1,0:T(8,128)} %reduce-scatter.5.cloned.1.call-done, bf16[128,2048]{1,0:T(8,128)(2,1)S(1)} %copy-done.2), kind=kLoop, calls=%fused_computation.26 | loop fusion | flops 2621440 | bytes 2097152 | tf_op jit(solution)/shard_map/convert_element_type | solution.py:55
  (4 shorter events, 0.0 us)
Async XLA Ops:
  7.2 41.1 %all-gather.3.cloned.1.call-start = ((), (), s32[]{:S(2)}) async-start(), calls=%async_computation.2 | async-start | bytes 2621440 | tf_op jit(solution)/shard_map/all_gather | solution.py:30
  9.3 69.8 %all-gather.5.cloned.1.call-start = ((), (), s32[]{:S(2)}) async-start(), calls=%async_computation.4 | async-start | bytes 2359296 | tf_op jit(solution)/shard_map/all_gather | solution.py:29
  10.0 120.8 %reduce-scatter.3.cloned.1.call-start = ((), (), s32[]{:S(2)}) async-start(), calls=%async_computation.3 | async-start | bytes 4718592 | tf_op jit(solution)/shard_map/reduce_scatter | solution.py:42
  55.2 2.0 %copy-start.1 = (bf16[1,1,8,256,256]{4,3,2,1,0:T(8,128)(2,1)S(1)}, bf16[1,1,8,256,256]{4,3,2,1,0:T(8,128)(2,1)}, u32[]{:S(2)}) copy-start(bf16[1,1,8,256,256]{4,3,2,1,0:T(8,128)(2,1)} %param.9) | copy-start | bytes 3145732
  75.5 109.1 %reduce-scatter.5.cloned.1.call-start = ((), (), s32[]{:S(2)}) async-start(), calls=%async_computation.5 | async-start | bytes 5242880 | tf_op jit(solution)/shard_map/reduce_scatter | solution.py:50
  105.9 1.6 copy-start
  107.5 77.1 %copy-start.2 = (bf16[128,2048]{1,0:T(8,128)(2,1)S(1)}, bf16[128,2048]{1,0:T(8,128)(2,1)}, u32[]{:S(2)}) copy-start(bf16[128,2048]{1,0:T(8,128)(2,1)} %param.8) | copy-start | bytes 1572868
Sparse Core Ops, SparseCore 0:
  10.4 37.8 all-gather.2
  49.9 29.0 all-gather.4
  81.3 49.4 reduce-scatter.2
  133.7 50.8 reduce-scatter.4
where the time goes:
time: 194 us
  waiting for transfers between devices  112 us (58%)
  local copies, waits for them, and re-layouts  36 us (19%)
  matrix products  21.5 us (11%)
  between operations  14.5 us (7%)
  other arithmetic  9.6 us (5%)
    reduce_scatter x1, waiting for transfers between devices, on_device(): lax.psum_scatter(placed.reshape(count, row_span * width), 'col', scatter_...  51.9 us
    all_gather x1, waiting for transfers between devices, on_device(): lax.all_gather(hidden_pre, 'col', axis=0, tiled=True)  36.2 us
    reduce_scatter x1, waiting for transfers between devices, on_device(): lax.psum_scatter(partial_value, 'row', scatter_dimension=0, tiled=True)  19.4 us
    unnamed x9, local copies, waits for them, and re-layouts  11.5 us
    transpose x1, local copies, waits for them, and re-layouts, on_device(): jnp.einsum('nkq,kpq->nkp', g_stack, w_live, preferred_element_type=jnp.fl...  5.48 us
    transpose x1, local copies, waits for them, and re-layouts, on_device(): jnp.einsum('nkp,kpq->nkq', a_stack, w_live, preferred_element_type=jnp.fl...  5.48 us
    dot_general x1, matrix products, on_device(): jnp.einsum('nkp,kpq->nkq', a_stack, w_live, preferred_element_type=jnp.fl...  4.6 us
    dot_general x1, matrix products, on_device(): jnp.einsum('nkq,kpq->nkp', g_stack, w_live, preferred_element_type=jnp.fl...  4.39 us
  transfers between devices with their start and end apart: 4, of which 4 were waited for; matrix products, arithmetic and copies ran while one was open for 32% of the time, Pallas kernels for 0%

commit v1 on v0

--- a/solution.py
+++ b/solution.py
@@ -26,7 +26,22 @@
     col_pick = (col_local[:, None] == jnp.arange(col_span, dtype=jnp.int32)[None, :]).astype(
         jnp.float32
     )
-    grad_full = lax.all_gather(out_grad, "row", axis=0, tiled=True)
+    size, index, rows = (lax.axis_size("row"), lax.axis_index("row"), out_grad.shape[0])
+    right = [(i, (i + 1) % size) for i in range(size)]
+    left = [(i, (i - 1) % size) for i in range(size)]
+    out = jnp.zeros((*out_grad.shape[:0], size * rows, *out_grad.shape[0 + 1 :]), out_grad.dtype)
+    out = lax.dynamic_update_slice_in_dim(out, out_grad, index * rows, axis=0)
+    from_left = from_right = out_grad
+    halfway = size // 2
+    for turn in range(1, halfway + 1):
+        from_left = lax.ppermute(from_left, "row", right)
+        out = lax.dynamic_update_slice_in_dim(out, from_left, (index - turn) % size * rows, axis=0)
+        if turn < size - halfway:
+            from_right = lax.ppermute(from_right, "row", left)
+            out = lax.dynamic_update_slice_in_dim(
+                out, from_right, (index + turn) % size * rows, axis=0
+            )
+    grad_full = out
     act_rows = silu_rounded(lax.all_gather(hidden_pre, "col", axis=0, tiled=True))
     count = act_rows.shape[0]
     a_stack = jnp.take(act_rows.reshape(count, row_span, width), row_local, axis=1)

time: 194 us -> 230 us (1.19)
  local copies, waits for them, and re-layouts: 36 us -> 69.3 us
  starting transfers between devices: 0.34 us -> 12.5 us
  waiting for transfers between devices: 112 us -> 104 us
    all_gather x1, waiting for transfers between devices: 36.2 us -> 0.02 us  [on_device(): lax.all_gather(hidden_pre, 'col', axis=0, tiled=True)]
    dynamic_update_slice x0 -> x8, local copies, waits for them, and re-layouts: none -> 35.6 us  [the longest x3 16.8 us: on_device(): lax.dynamic_update_slice_in_dim(out, from_right, (index + turn) % size *...]
    reduce_scatter x1, waiting for transfers between devices: 19.4 us -> 50 us  [on_device(): lax.psum_scatter(partial_value, 'row', scatter_dimension=0, tiled=True)]
    ppermute x0 -> x7, waiting for transfers between devices: none -> 25.3 us  [the longest x4 23.5 us: on_device(): from_left = lax.ppermute(from_left, 'row', right)]
    reduce_scatter x1, waiting for transfers between devices: 51.9 us -> 29 us  [on_device(): lax.psum_scatter(placed.reshape(count, row_span * width), 'col', scatter_...]
    ppermute x0 -> x7, starting transfers between devices: none -> 12.2 us  [the longest x3 11.7 us: on_device(): from_right = lax.ppermute(from_right, 'row', left)]
    all_gather x1 -> x0, local copies, waits for them, and re-layouts: 3.91 us -> none  [on_device(): grad_full = lax.all_gather(out_grad, 'row', axis=0, tiled=True)]
    all_gather x1 -> x0, waiting for transfers between devices: 3.26 us -> none  [on_device(): grad_full = lax.all_gather(out_grad, 'row', axis=0, tiled=True)]
  transfers between devices with their start and end apart: 4 -> 10, of which waited for: 4 -> 7; matrix products, arithmetic and copies ran while one was open for 32% -> 40% of each run, Pallas kernels for 0% -> 0%
where the time goes in v1:
time: 230 us; the launch traced here: 229 us
  waiting for transfers between devices  104 us (45%)
  local copies, waits for them, and re-layouts  69.3 us (30%)
  matrix products  19.6 us (9%)
  between operations  14.8 us (6%)
  starting transfers between devices  12.5 us (5%)
  other arithmetic  8.29 us (4%)
    reduce_scatter x1, waiting for transfers between devices, on_device(): lax.psum_scatter(partial_value, 'row', scatter_dimension=0, tiled=True)  50 us
    reduce_scatter x1, waiting for transfers between devices, on_device(): lax.psum_scatter(placed.reshape(count, row_span * width), 'col', scatter_...  29 us
    ppermute x4, waiting for transfers between devices, on_device(): from_left = lax.ppermute(from_left, 'row', right)  23.5 us
    dynamic_update_slice x3, local copies, waits for them, and re-layouts, on_device(): lax.dynamic_update_slice_in_dim(out, from_right, (index + turn) % size *...  16.8 us
    dynamic_update_slice x4, local copies, waits for them, and re-layouts, on_device(): lax.dynamic_update_slice_in_dim(out, from_left, (index - turn) % size * r...  16.4 us
    unnamed x22, local copies, waits for them, and re-layouts  12.9 us
    ppermute x3, starting transfers between devices, on_device(): from_right = lax.ppermute(from_right, 'row', left)  11.7 us
    transpose x1, local copies, waits for them, and re-layouts, on_device(): jnp.einsum('nkp,kpq->nkq', a_stack, w_live, preferred_element_type=jnp.fl...  5.53 us
  transfers between devices with their start and end apart: 10, of which 7 were waited for; matrix products, arithmetic and copies ran while one was open for 40% of the time, Pallas kernels for 0%

profile of v1, /device:TPU:0, one launch (start us, length us, event | category | flops | bytes accessed | tf_op | source)
XLA Modules:
  0.0 228.9 jit_solution(7013939721395687357)
XLA Ops:
  7.2 0.0 all-gather.2.cloned.1.call-start
  7.2 2.0 copy.10
  9.3 0.0 all-gather.2.cloned.1.call-update
  9.3 0.0 copy-start.8
  9.3 0.0 reduce-scatter.5.cloned.1.call-start
  9.3 1.2 copy.14
  10.6 0.5 collective-permute-start
  11.1 4.1 %collective-permute-start.1 = (bf16[64,2048]{0,1:T(8,128)(2,1)S(1)}, bf16[64,2048]{0,1:T(8,128)(2,1)S(1)}, u32[]{:S(2)}, u32[]{:S(2)}) collective-permute-start(bf16[64,2048]{0,1:T(8,128)(2,1)S(1)} %copy.14), channel_id=1, source_target_pairs={{0,28},{4,0},{8,4},{12,8},{16,12},{20,16},{24,20},{28,24},{1,29},{... | collective-permute-start | bytes 786440 | tf_op jit(solution)/shard_map/ppermute | solution.py:40
  15.2 9.8 %collective-permute-done = bf16[64,2048]{0,1:T(8,128)(2,1)S(1)} collective-permute-done((bf16[64,2048]{0,1:T(8,128)(2,1)S(1)}, bf16[64,2048]{0,1:T(8,128)(2,1)S(1)}, u32[]{:S(2)}, u32[]{:S(2)}) %collective-permute-start) | collective-permute-done | bytes 262176 | tf_op jit(solution)/shard_map/ppermute | solution.py:37
  24.9 0.5 collective-permute-done.1
  25.4 3.8 %collective-permute-start.3 = (bf16[64,2048]{0,1:T(8,128)(2,1)S(1)}, bf16[64,2048]{0,1:T(8,128)(2,1)}, u32[]{:S(2)}, u32[]{:S(2)}) collective-permute-start(bf16[64,2048]{0,1:T(8,128)(2,1)S(1)} %collective-permute-done.1), channel_id=1, source_target_pairs={{0,28},{4,0},{8,4},{12,8},{16,12},{20,16},{24,20},{28,24},{1,29},{... | collective-permute-start | bytes 786440 | tf_op jit(solution)/shard_map/ppermute | solution.py:40
  29.3 8.2 %collective-permute-done.2 = bf16[64,2048]{0,1:T(8,128)(2,1)S(1)} collective-permute-done((bf16[64,2048]{0,1:T(8,128)(2,1)S(1)}, bf16[64,2048]{0,1:T(8,128)(2,1)S(1)}, u32[]{:S(2)}, u32[]{:S(2)}) %collective-permute-start.2) | collective-permute-done | bytes 262176 | tf_op jit(solution)/shard_map/ppermute | solution.py:37
  37.5 1.2 collective-permute-done.3
  38.7 3.8 %collective-permute-start.5 = (bf16[64,2048]{0,1:T(8,128)(2,1)}, bf16[64,2048]{0,1:T(8,128)(2,1)}, u32[]{:S(2)}, u32[]{:S(2)}) collective-permute-start(bf16[64,2048]{0,1:T(8,128)(2,1)} %collective-permute-done.3), channel_id=1, source_target_pairs={{0,28},{4,0},{8,4},{12,8},{16,12},{20,16},{24,20},{28,24},{1,29},{... | collective-permute-start | bytes 786440 | tf_op jit(solution)/shard_map/ppermute | solution.py:40
  42.5 5.6 %collective-permute-done.4 = bf16[64,2048]{0,1:T(8,128)(2,1)} collective-permute-done((bf16[64,2048]{0,1:T(8,128)(2,1)S(1)}, bf16[64,2048]{0,1:T(8,128)(2,1)}, u32[]{:S(2)}, u32[]{:S(2)}) %collective-permute-start.4) | collective-permute-done | bytes 262176 | tf_op jit(solution)/shard_map/ppermute | solution.py:37
  48.1 0.0 collective-permute-start.6
  48.9 0.1 broadcast_in_dim.43
  49.1 2.4 %dynamic_update_slice.24 = bf16[512,2048]{0,1:T(8,128)(2,1)S(1)} dynamic-update-slice(bf16[512,2048]{0,1:T(8,128)(2,1)S(1)} %broadcast_in_dim.43, bf16[64,2048]{0,1:T(8,128)(2,1)S(1)} %copy.14, s32[]{:T(128)S(6)} %select_n.71, s32[]{:T(128)} %constant.75.clone.1) | dynamic-update-slice | bytes 524292 | tf_op jit(solution)/shard_map/dynamic_update_slice | solution.py:33
  51.5 3.6 %dynamic_update_slice.25 = bf16[512,2048]{0,1:T(8,128)(2,1)S(1)} dynamic-update-slice(bf16[512,2048]{0,1:T(8,128)(2,1)S(1)} %dynamic_update_slice.24, bf16[64,2048]{0,1:T(8,128)(2,1)S(1)} %collective-permute-done, s32[]{:T(128)S(6)} %select_n.73, s32[]{:T(128)} %constant.75.clone.1) | dynamic-update-slice | bytes 524292 | tf_op jit(solution)/shard_map/dynamic_update_slice | solution.py:38
  55.2 5.9 %dynamic_update_slice.26 = bf16[512,2048]{0,1:T(8,128)(2,1)S(1)} dynamic-update-slice(bf16[512,2048]{0,1:T(8,128)(2,1)S(1)} %dynamic_update_slice.25, bf16[64,2048]{0,1:T(8,128)(2,1)} %copy-done.4, s32[]{:T(128)S(6)} %select_n.75, s32[]{:T(128)} %constant.75.clone.1) | dynamic-update-slice | bytes 524292 | tf_op jit(solution)/shard_map/dynamic_update_slice | solution.py:41
  61.1 2.0 dynamic_update_slice.27
  63.1 4.9 %dynamic_update_slice.28 = bf16[512,2048]{0,1:T(8,128)(2,1)S(1)} dynamic-update-slice(bf16[512,2048]{0,1:T(8,128)(2,1)S(1)} %dynamic_update_slice.27, bf16[64,2048]{0,1:T(8,128)(2,1)} %collective-permute-done.3, s32[]{:T(128)S(6)} %select_n.79, s32[]{:T(128)} %constant.75.clone.1) | dynamic-update-slice | bytes 524292 | tf_op jit(solution)/shard_map/dynamic_update_slice | solution.py:41
  68.0 5.9 %dynamic_update_slice.29 = bf16[512,2048]{0,1:T(8,128)(2,1)S(1)} dynamic-update-slice(bf16[512,2048]{0,1:T(8,128)(2,1)S(1)} %dynamic_update_slice.28, bf16[64,2048]{0,1:T(8,128)(2,1)} %collective-permute-done.4, s32[]{:T(128)S(6)} %select_n.81, s32[]{:T(128)} %constant.75.clone.1) | dynamic-update-slice | bytes 524292 | tf_op jit(solution)/shard_map/dynamic_update_slice | solution.py:38
  74.0 5.9 %dynamic_update_slice.30 = bf16[512,2048]{0,1:T(8,128)(2,1)S(1)} dynamic-update-slice(bf16[512,2048]{0,1:T(8,128)(2,1)S(1)} %dynamic_update_slice.29, bf16[64,2048]{0,1:T(8,128)(2,1)} %collective-permute-done.5, s32[]{:T(128)S(6)} %select_n.83, s32[]{:T(128)} %constant.75.clone.1) | dynamic-update-slice | bytes 524292 | tf_op jit(solution)/shard_map/dynamic_update_slice | solution.py:41
  79.9 4.9 %dynamic_update_slice.31 = bf16[512,2048]{0,1:T(8,128)(2,1)S(1)} dynamic-update-slice(bf16[512,2048]{0,1:T(8,128)(2,1)S(1)} %dynamic_update_slice.30, bf16[64,2048]{0,1:T(8,128)(2,1)} %collective-permute-done.6, s32[]{:T(128)S(6)} %select_n.85, s32[]{:T(128)} %constant.75.clone.1) | dynamic-update-slice | bytes 524292 | tf_op jit(solution)/shard_map/dynamic_update_slice | solution.py:38
  84.8 2.4 %copy.17 = bf16[512,8,256]{2,0,1:T(8,128)(2,1)} copy(bf16[512,8,256]{0,2,1:T(8,128)(2,1)S(1)} %bitcast.52) | data formatting | bytes 4194304 | tf_op jit(solution)/shard_map/reshape | solution.py:62
  87.2 2.4 %gather_fusion.1 = bf16[8,512,256]{2,1,0:T(8,128)(2,1)S(1)} fusion(bf16[512,8,256]{2,0,1:T(8,128)(2,1)} %copy.17, s32[1024]{0:T(1024)S(1)} %pad_clamp_fusion), kind=kCustom, calls=%fused_computation.1.clone | custom fusion | bytes 4194336 | tf_op jit(solution)/shard_map/jit(_take)/gather | solution.py:62
  89.6 2.8 %convolution_bitcast_fusion = f32[512,8,256]{0,2,1:T(8,128)} fusion(bf16[8,512,256]{2,1,0:T(8,128)(2,1)S(1)} %gather_fusion.1, pred[8]{0:T(512)(128)(4,1)S(1)} %get-tuple-element.4, bf16[1,1,8,256,256]{4,3,2,1,0:T(8,128)(2,1)S(1)} %copy-done.2, pred[8]{0:T(512)(128)(4,1)S(1)} %get-tuple-element.8), kind=kOutput, calls=%fused_computation.8 | convolution fusion | flops 538443776 | bytes 7340048 | tf_op jit(solution)/shard_map/nkq,kpq->nkp/dot_general | solution.py:63
  92.4 5.5 %copy.18 = f32[512,8,256]{2,1,0:T(8,128)} copy(f32[512,8,256]{0,2,1:T(8,128)} %convolution_bitcast_fusion) | data formatting | bytes 8388608 | tf_op jit(solution)/shard_map/nkq,kpq->nkp/transpose | solution.py:63
  97.9 4.2 %fusion.24 = f32[8,512,256]{2,0,1:T(8,128)S(1)} fusion(f32[512,8,256]{2,1,0:T(8,128)} %copy.18, s32[8]{0:T(128)S(1)} %get-tuple-element.7), kind=kOutput, calls=%fused_computation.35 | convolution fusion | flops 100663360 | bytes 8388640 | tf_op jit(solution)/shard_map/nkp,kr->nrp/dot_general | solution.py:64
  102.1 3.9 %copy.23 = f32[64,8,8,256]{3,1,2,0:T(8,128)} copy(f32[64,8,8,256]{3,2,1,0:T(8,128)S(1)} %bitcast.51) | data formatting | bytes 8388608
  106.0 0.0 reduce-scatter.5.cloned.1.call-update
  106.0 0.2 reduce-scatter.3.cloned.1.call-start
  106.3 0.0 all-gather.2.cloned.1.call-done
  106.3 4.1 %fusion.3 = bf16[512,2048]{0,1:T(8,128)(2,1)} fusion(bf16[512,2048]{0,1:T(8,128)(2,1)} %all-gather.2.cloned.1.call-done), kind=kLoop, calls=%fused_computation.7 | loop fusion | flops 6291456 | bytes 4194304 | tf_op jit(solution)/shard_map/convert_element_type | solution.py:8
  110.4 2.8 %copy.11 = bf16[512,8,256]{2,0,1:T(8,128)(2,1)S(1)} copy(bf16[512,8,256]{0,2,1:T(8,128)(2,1)} %bitcast.53) | data formatting | bytes 4194304 | tf_op jit(solution)/shard_map/reshape | solution.py:47
  113.2 2.0 gather_fusion
  115.2 4.5 %convolution_bitcast_fusion.1 = f32[512,8,256]{0,2,1:T(8,128)} fusion(bf16[8,512,256]{2,1,0:T(8,128)(2,1)} %gather_fusion, pred[8]{0:T(512)(128)(4,1)S(1)} %get-tuple-element.6, bf16[1,1,8,256,256]{4,3,2,1,0:T(8,128)(2,1)S(1)} %copy-done.2, pred[8]{0:T(512)(128)(4,1)S(1)} %get-tuple-element.8), kind=kOutput, calls=%fused_computation.9 | convolution fusion | flops 538443776 | bytes 7340048 | tf_op jit(solution)/shard_map/nkp,kpq->nkq/dot_general | solution.py:48
  119.7 5.5 %copy.13 = f32[512,8,256]{2,1,0:T(8,128)} copy(f32[512,8,256]{0,2,1:T(8,128)} %convolution_bitcast_fusion.1) | data formatting | bytes 8388608 | tf_op jit(solution)/shard_map/nkp,kpq->nkq/transpose | solution.py:48
  125.2 4.2 %fusion.21 = f32[8,512,256]{2,0,1:T(8,128)S(1)} fusion(f32[512,8,256]{2,1,0:T(8,128)} %copy.13, s32[8]{0:T(128)S(1)} %get-tuple-element.5), kind=kOutput, calls=%fused_computation.33 | convolution fusion | flops 100663360 | bytes 8388640 | tf_op jit(solution)/shard_map/nkq,kc->ncq/dot_general | solution.py:49
  129.5 3.9 %copy.22 = f32[64,8,8,256]{3,1,2,0:T(8,128)} copy(f32[64,8,8,256]{3,2,1,0:T(8,128)S(1)} %bitcast.50) | data formatting | bytes 8388608
  133.4 0.0 reduce-scatter.3.cloned.1.call-update
  133.4 1.8 copy-done.1
  135.2 4.0 %select_bitcast_fusion = f32[1,1,8,256,256]{4,3,2,1,0:T(8,128)} fusion(pred[8]{0:T(512)(128)(4,1)S(1)} %get-tuple-element.8, bf16[8,512,256]{2,1,0:T(8,128)(2,1)} %gather_fusion, pred[8]{0:T(512)(128)(4,1)S(1)} %get-tuple-element.6, bf16[8,512,256]{2,1,0:T(8,128)(2,1)S(1)} %copy-done.1, pred[8]{0:T(512)(128)(4,1)S(1)} %get-tuple-element.4), kind=kOutput, calls=%fused_computation.15 | convolution fusion | flops 539492352 | bytes 6291480 | tf_op jit(solution)/shard_map/nkp,nkq->kpq/dot_general | solution.py:56
  139.2 29.0 %reduce-scatter.5.cloned.1.call-done = f32[128,2048]{1,0:T(8,128)} async-done(((f32[512,2048]{1,0:T(8,128)}), f32[128,2048]{1,0:T(8,128)}) %reduce-scatter.5.cloned.1.call-update) | async-done | bytes 1048592 | tf_op jit(solution)/shard_map/reduce_scatter | solution.py:65
  168.2 2.4 %fusion.19 = bf16[128,2048]{1,0:T(8,128)(2,1)} fusion(f32[128,2048]{1,0:T(8,128)} %reduce-scatter.5.cloned.1.call-done, bf16[128,2048]{1,0:T(8,128)(2,1)S(1)} %copy-done.3), kind=kLoop, calls=%fused_computation.26 | loop fusion | flops 2621440 | bytes 2097152 | tf_op jit(solution)/shard_map/convert_element_type | solution.py:70
  170.6 50.0 %reduce-scatter.3.cloned.1.call-done = f32[64,2048]{1,0:T(8,128)} async-done(((f32[512,2048]{1,0:T(8,128)}), f32[64,2048]{1,0:T(8,128)}) %reduce-scatter.3.cloned.1.call-update) | async-done | bytes 524304 | tf_op jit(solution)/shard_map/reduce_scatter | solution.py:57
  220.6 1.8 convert_element_type.21
  (26 shorter events, 0.1 us)
Async XLA Ops:
  7.2 30.3 %copy-start.7 = (s32[1,1,8]{2,1,0:T(1,128)S(1)}, s32[1,1,8]{2,1,0:T(1,128)}, u32[]{:S(2)}) copy-start(s32[1,1,8]{2,1,0:T(1,128)} %param.11) | copy-start | bytes 100
  7.2 99.1 %all-gather.2.cloned.1.call-start = ((), (), s32[]{:S(2)}) async-start(), calls=%async_computation.2 | async-start | bytes 2621440 | tf_op jit(solution)/shard_map/all_gather | solution.py:45
  9.3 42.2 %copy-start.8 = (s32[1,1,8]{2,1,0:T(1,128)S(1)}, s32[1,1,8]{2,1,0:T(1,128)}, u32[]{:S(2)}) copy-start(s32[1,1,8]{2,1,0:T(1,128)} %param.10) | copy-start | bytes 100
  9.3 158.9 %reduce-scatter.5.cloned.1.call-start = ((), (), s32[]{:S(2)}) async-start(), calls=%async_computation.4 | async-start | bytes 5242880 | tf_op jit(solution)/shard_map/reduce_scatter | solution.py:65
  10.6 14.4 %collective-permute-start = (bf16[64,2048]{0,1:T(8,128)(2,1)S(1)}, bf16[64,2048]{0,1:T(8,128)(2,1)S(1)}, u32[]{:S(2)}, u32[]{:S(2)}) collective-permute-start(bf16[64,2048]{0,1:T(8,128)(2,1)S(1)} %copy.14), channel_id=1, source_target_pairs={{0,4},{4,8},{8,12},{12,16},{16,20},{20,24},{24,28},{28,0},{1,5},{5... | collective-permute-start | bytes 786440 | tf_op jit(solution)/shard_map/ppermute | solution.py:37
  11.1 14.4 %collective-permute-start.1 = (bf16[64,2048]{0,1:T(8,128)(2,1)S(1)}, bf16[64,2048]{0,1:T(8,128)(2,1)S(1)}, u32[]{:S(2)}, u32[]{:S(2)}) collective-permute-start(bf16[64,2048]{0,1:T(8,128)(2,1)S(1)} %copy.14), channel_id=1, source_target_pairs={{0,28},{4,0},{8,4},{12,8},{16,12},{20,16},{24,20},{28,24},{1,29},{... | collective-permute-start | bytes 786440 | tf_op jit(solution)/shard_map/ppermute | solution.py:40
  24.9 12.5 %collective-permute-start.2 = (bf16[64,2048]{0,1:T(8,128)(2,1)S(1)}, bf16[64,2048]{0,1:T(8,128)(2,1)S(1)}, u32[]{:S(2)}, u32[]{:S(2)}) collective-permute-start(bf16[64,2048]{0,1:T(8,128)(2,1)S(1)} %collective-permute-done), channel_id=1, source_target_pairs={{0,4},{4,8},{8,12},{12,16},{16,20},{20,24},{24,28},{28,0},{1,5},{5... | collective-permute-start | bytes 786440 | tf_op jit(solution)/shard_map/ppermute | solution.py:37
  25.4 23.5 %copy-start.4 = (bf16[64,2048]{0,1:T(8,128)(2,1)}, bf16[64,2048]{0,1:T(8,128)(2,1)S(1)}, u32[]{:S(2)}) copy-start(bf16[64,2048]{0,1:T(8,128)(2,1)S(1)} %collective-permute-done.1) | copy-start | bytes 786436
  25.4 13.2 %collective-permute-start.3 = (bf16[64,2048]{0,1:T(8,128)(2,1)S(1)}, bf16[64,2048]{0,1:T(8,128)(2,1)}, u32[]{:S(2)}, u32[]{:S(2)}) collective-permute-start(bf16[64,2048]{0,1:T(8,128)(2,1)S(1)} %collective-permute-done.1), channel_id=1, source_target_pairs={{0,28},{4,0},{8,4},{12,8},{16,12},{20,16},{24,20},{28,24},{1,29},{... | collective-permute-start | bytes 786440 | tf_op jit(solution)/shard_map/ppermute | solution.py:40
  37.4 11.5 %copy-start.5 = (bf16[64,2048]{0,1:T(8,128)(2,1)}, bf16[64,2048]{0,1:T(8,128)(2,1)S(1)}, u32[]{:S(2)}) copy-start(bf16[64,2048]{0,1:T(8,128)(2,1)S(1)} %collective-permute-done.2) | copy-start | bytes 786436
  37.4 10.7 %collective-permute-start.4 = (bf16[64,2048]{0,1:T(8,128)(2,1)S(1)}, bf16[64,2048]{0,1:T(8,128)(2,1)}, u32[]{:S(2)}, u32[]{:S(2)}) collective-permute-start(bf16[64,2048]{0,1:T(8,128)(2,1)S(1)} %collective-permute-done.2), channel_id=1, source_target_pairs={{0,4},{4,8},{8,12},{12,16},{16,20},{20,24},{24,28},{28,0},{1,5},{5... | collective-permute-start | bytes 786440 | tf_op jit(solution)/shard_map/ppermute | solution.py:37
  38.7 35.3 %collective-permute-start.5 = (bf16[64,2048]{0,1:T(8,128)(2,1)}, bf16[64,2048]{0,1:T(8,128)(2,1)}, u32[]{:S(2)}, u32[]{:S(2)}) collective-permute-start(bf16[64,2048]{0,1:T(8,128)(2,1)} %collective-permute-done.3), channel_id=1, source_target_pairs={{0,28},{4,0},{8,4},{12,8},{16,12},{20,16},{24,20},{28,24},{1,29},{... | collective-permute-start | bytes 786440 | tf_op jit(solution)/shard_map/ppermute | solution.py:40
  48.1 31.8 %collective-permute-start.6 = (bf16[64,2048]{0,1:T(8,128)(2,1)}, bf16[64,2048]{0,1:T(8,128)(2,1)}, u32[]{:S(2)}, u32[]{:S(2)}) collective-permute-start(bf16[64,2048]{0,1:T(8,128)(2,1)} %collective-permute-done.4), channel_id=1, source_target_pairs={{0,4},{4,8},{8,12},{12,16},{16,20},{20,24},{24,28},{28,0},{1,5},{5... | collective-permute-start | bytes 786440 | tf_op jit(solution)/shard_map/ppermute | solution.py:37
  51.4 9.7 %copy-start.6 = (bf16[64,2048]{0,1:T(8,128)(2,1)S(1)}, bf16[64,2048]{0,1:T(8,128)(2,1)}, u32[]{:S(2)}) copy-start(bf16[64,2048]{0,1:T(8,128)(2,1)} %copy-done.5) | copy-start | bytes 786436
  87.2 2.4 %copy-start.2 = (bf16[1,1,8,256,256]{4,3,2,1,0:T(8,128)(2,1)S(1)}, bf16[1,1,8,256,256]{4,3,2,1,0:T(8,128)(2,1)}, u32[]{:S(2)}) copy-start(bf16[1,1,8,256,256]{4,3,2,1,0:T(8,128)(2,1)} %param.9) | copy-start | bytes 3145732
  89.6 2.8 %copy-start = (bf16[8,512,256]{2,1,0:T(8,128)(2,1)}, bf16[8,512,256]{2,1,0:T(8,128)(2,1)S(1)}, u32[]{:S(2)}) copy-start(bf16[8,512,256]{2,1,0:T(8,128)(2,1)S(1)} %gather_fusion.1) | copy-start | bytes 6291460
  106.0 114.5 %reduce-scatter.3.cloned.1.call-start = ((), (), s32[]{:S(2)}) async-start(), calls=%async_computation.3 | async-start | bytes 4718592 | tf_op jit(solution)/shard_map/reduce_scatter | solution.py:57
  133.4 1.8 copy-start.1
  135.2 32.9 %copy-start.3 = (bf16[128,2048]{1,0:T(8,128)(2,1)S(1)}, bf16[128,2048]{1,0:T(8,128)(2,1)}, u32[]{:S(2)}) copy-start(bf16[128,2048]{1,0:T(8,128)(2,1)} %param.8) | copy-start | bytes 1572868
Sparse Core Ops, SparseCore 0:
  10.4 37.8 all-gather.1
  106.2 61.9 reduce-scatter.4
  170.6 49.9 reduce-scatter.2
